TPU v7x, 32 devices: a whole 2x2x4 slice. The times are simulated.
32 devices in a mesh: grp: 4 (over z), shard: 8 (over y, x, core).
Axes of the slice: x: 2, y: 2, z: 4, core: 2. Of those that a mesh axis runs over, the one named last changes fastest.
Arguments:
- activations: bfloat16 [256, 5120], P('grp', 'shard'), may hold values from -6 to 6
- grad_outputs: bfloat16 [256, 27648], P('shard', 'grp'), may hold values from -6 to 6
- basis_in: bfloat16 [5120, 2560], P('shard', 'grp'), may hold values from -0.078125 to 0.078125
- basis_out: bfloat16 [27648, 13824], P('grp', 'shard'), may hold values from -0.0390625 to 0.0390625
- query_grads: bfloat16 [4, 2560, 13824], P('grp', None, 'shard'), may hold values from -0.0009765625 to 0.0009765625
Outputs:
- scores: float32 [4, 256], P('grp', 'shard')
All inputs are finite; a program needn't handle non-finite values.
Results may differ from a plain program's by a relative error of at most 0.0041.
Values may be sent and summed in bfloat16 or wider, within the bound.
A program may use at most 128 MiB of HBM per device.

v0:
```python
import jax
import jax.numpy as jnp
from jax import lax
from jax.sharding import PartitionSpec as P


def local(activations, grad_outputs, basis_in, basis_out, query_grads):
    full_in = lax.all_gather(basis_in, "grp", axis=1, tiled=True)
    act_terms = lax.dot_general(
        full_in, activations, (((0,), (1,)), ((), ())), preferred_element_type=jnp.float32
    )
    act_local = lax.psum(act_terms, "shard").astype(jnp.bfloat16)
    act_rot = lax.all_gather(act_local, "grp", axis=1, tiled=True)
    out_terms = jnp.dot(
        lax.all_gather(grad_outputs, "shard", axis=0, tiled=True),
        basis_out,
        preferred_element_type=jnp.float32,
    )
    out_rot = lax.psum(out_terms, "grp").astype(jnp.bfloat16)
    mixed = lax.dot_general(
        act_rot, query_grads[0], (((0,), (0,)), ((), ())), preferred_element_type=jnp.float32
    )
    partial_scores = jnp.sum(mixed * out_rot.astype(jnp.float32), axis=1)
    return lax.psum_scatter(partial_scores[None, :], "shard", scatter_dimension=1, tiled=True)


def solution(mesh):
    placed = (
        P("grp", "shard"),
        P("shard", "grp"),
        P("shard", "grp"),
        P("grp", "shard"),
        P("grp", None, "shard"),
    )
    return jax.shard_map(
        local, mesh=mesh, in_specs=placed, out_specs=P("grp", "shard"), check_vma=False
    )
```

profile of v0, /device:TPU:0, one launch (start us, length us, event | category | flops | bytes accessed | tf_op | source)
XLA Modules:
  0.0 259.3 jit_solution(14320532215565623400)
XLA Ops:
  6.5 0.0 copy-start
  6.5 0.0 all-gather.4.cloned.1.call-start
  6.5 0.7 all-gather.4.cloned.1.call-update
  7.3 0.0 all-gather.8.cloned.1.call-start
  7.3 0.7 all-gather.8.cloned.1.call-update
  8.0 0.0 all-gather.6.cloned.1.call-start
  8.1 69.2 %all-gather.4.cloned.1.call-done = bf16[640,2560]{1,0:T(8,128)(2,1)} async-done(((bf16[640,640]{1,0:T(8,128)(2,1)}), bf16[640,2560]{1,0:T(8,128)(2,1)}) %all-gather.4.cloned.1.call-update) | async-done | bytes 3276816 | tf_op jit(solution)/shard_map/all_gather | solution.py:8
  77.2 0.0 copy-done
  77.2 2.6 %fusion.9 = f32[2560,64]{0,1:T(8,128)S(1)} fusion(bf16[64,640]{1,0:T(8,128)(2,1)S(1)} %copy-done, bf16[640,2560]{1,0:T(8,128)(2,1)} %all-gather.4.cloned.1.call-done), kind=kOutput, calls=%fused_computation.5 | convolution fusion | flops 209715200 | bytes 4014080 | tf_op jit(solution)/shard_map/dot_general | solution.py:9
  79.9 36.6 %all-reduce.3 = bf16[2560,64]{0,1:T(8,128)(2,1)} all-reduce(f32[2560,64]{0,1:T(8,128)S(1)} %fusion.9), channel_id=1, replica_groups=mesh['grp'=4,'shard'=8] {'shard'}, use_global_device_ids=true, to_apply=%region_0.0 | all-reduce | flops 163840 | bytes 983040 | tf_op jit(solution)/shard_map/psum | solution.py:12
  116.4 0.0 all-gather.6.cloned.1.call-update
  116.5 0.0 reduce-scatter.4.cloned.1.call-start
  116.5 1.6 all-gather.8.cloned.1.call-done
  118.1 12.4 %fusion.8 = f32[256,1728]{0,1:T(8,128)S(1)} fusion(bf16[256,6912]{1,0:T(8,128)(2,1)} %all-gather.8.cloned.1.call-done, bf16[6912,1728]{0,1:T(8,128)(2,1)} %param.8), kind=kOutput, calls=%fused_computation.4 | convolution fusion | flops 6115295232 | bytes 29196288 | tf_op jit(solution)/shard_map/dot_general | solution.py:14
  130.5 79.8 %all-reduce.2 = bf16[256,1728]{0,1:T(8,128)(2,1)S(1)} all-reduce(f32[256,1728]{0,1:T(8,128)S(1)} %fusion.8), channel_id=1, replica_groups=mesh['grp'=4,'shard'=8] {'grp'}, use_global_device_ids=true, to_apply=%region_1.0 | all-reduce | flops 442368 | bytes 2654208 | tf_op jit(solution)/shard_map/psum | solution.py:19
  210.3 0.0 all-gather.6.cloned.1.call-done
  210.4 6.4 %fusion.5 = f32[256]{0:T(256)S(1)} fusion(bf16[2560,256]{0,1:T(8,128)(2,1)} %all-gather.6.cloned.1.call-done, bf16[1,2560,1728]{1,2,0:T(8,128)(2,1)} %param.9, bf16[256,1728]{0,1:T(8,128)(2,1)S(1)} %all-reduce.2), kind=kOutput, calls=%fused_computation.3 | convolution fusion | flops 2266251008 | bytes 11043840 | tf_op jit(solution)/shard_map/dot_general | solution.py:20
  216.8 0.8 copy.6
  217.6 0.0 reduce-scatter.4.cloned.1.call-update
  217.6 33.8 %reduce-scatter.4.cloned.1.call-done = f32[32,1]{1,0:T(8,128)} async-done(((f32[256,1]{1,0:T(8,128)}), f32[32,1]{1,0:T(8,128)}) %reduce-scatter.4.cloned.1.call-update) | async-done | bytes 144
  251.4 1.3 copy.7
Async XLA Ops:
  6.5 70.7 %copy-start = (bf16[64,640]{1,0:T(8,128)(2,1)S(1)}, bf16[64,640]{1,0:T(8,128)(2,1)}, u32[]{:S(2)}) copy-start(bf16[64,640]{1,0:T(8,128)(2,1)} %param.5) | copy-start | bytes 245764
  6.5 70.7 %all-gather.4.cloned.1.call-start = ((), (), s32[]{:S(2)}) async-start(), calls=%async_computation.1 | async-start | bytes 4096000 | tf_op jit(solution)/shard_map/all_gather | solution.py:8
  7.3 110.8 %all-gather.8.cloned.1.call-start = ((), (), s32[]{:S(2)}) async-start(), calls=%async_computation.3 | async-start | bytes 3981312 | tf_op jit(solution)/shard_map/all_gather | solution.py:15
  8.0 202.3 %all-gather.6.cloned.1.call-start = ((), (), s32[]{:S(2)}) async-start(), calls=%async_computation.2 | async-start | bytes 1638400 | tf_op jit(solution)/shard_map/all_gather | solution.py:13
  116.5 135.0 %reduce-scatter.4.cloned.1.call-start = ((), (), s32[]{:S(2)}) async-start(), calls=%async_computation.4 | async-start | bytes 147456
Sparse Core Ops, SparseCore 0:
  8.9 68.2 all-gather.3
  79.1 38.9 all-gather.7
  119.7 46.3 all-gather.5
  217.7 33.6 reduce-scatter.3
where the time goes:
time: 260 us; the launch traced here: 259 us
  blocking collectives  116 us (45%)
  waiting for transfers between devices  106 us (41%)
  matrix products  21.5 us (8%)
  between operations  13.2 us (5%)
    psum x1, blocking collectives, local(): out_rot = lax.psum(out_terms, 'grp').astype(jnp.bfloat16)  79.8 us
    all_gather x1, waiting for transfers between devices, local(): full_in = lax.all_gather(basis_in, 'grp', axis=1, tiled=True)  69.2 us
    psum x1, blocking collectives, local(): act_local = lax.psum(act_terms, 'shard').astype(jnp.bfloat16)  36.6 us
    unnamed x5, waiting for transfers between devices  35.3 us
    dot_general x1, matrix products, local(): jnp.dot(lax.all_gather(grad_outputs, 'shard', axis=0, tiled=True), basis_...  12.4 us
    dot_general x1, matrix products, local(): lax.dot_general(act_rot, query_grads[0], (((0,), (0,)), ((), ())), prefer...  6.43 us
  transfers between devices with their start and end apart: 4, of which 3 were waited for; matrix products, arithmetic and copies ran while one was open for 6% of the time, Pallas kernels for 0%

commit v1 on v0

v1 whole, which is shorter than its diff:
```python
import functools

import jax
import jax.numpy as jnp
from jax import lax
from jax.experimental import pallas as pl
from jax.experimental.pallas import tpu as pltpu
from jax.sharding import PartitionSpec as P

F32, BF16 = jnp.float32, jnp.bfloat16
ROWS = 144
SKEW = 2
NT = (((1,), (1,)), ((), ()))


def remote(src, dst, send, recv, where):
    return pltpu.make_async_remote_copy(
        src_ref=src, dst_ref=dst, send_sem=send, recv_sem=recv,
        device_id=where, device_id_type=pl.DeviceIdType.MESH,
    )


def kernel(ng, ns, act, grad, bin_hbm, bout_hbm, query_hbm, score,
           bin_v, bout, query, abuf, tsend, tland, piece, arow, afull, gbuf,
           mixed, own, from_left, from_right, to_right, to_left, psend, pland,
           lsem, a_s, a_r, t_s, t_r, p_s, p_r, f_s, f_r, g_s, g_r,
           zr_s, zr_r, zl_s, zl_r, s_s, s_r):
    g, s = lax.axis_index("grp"), lax.axis_index("shard")
    chips = ns // 2
    chip, core = s // 2, s % 2
    sib = chip * 2 + 1 - core
    nch = own.shape[0]
    tok, width = abuf.shape[0] * abuf.shape[1], bin_v.shape[1]

    local = [
        pltpu.make_async_copy(bin_hbm, bin_v, lsem.at[0]),
        pltpu.make_async_copy(act, abuf.at[g], lsem.at[1]),
        pltpu.make_async_copy(grad, gbuf.at[s], lsem.at[2]),
        pltpu.make_async_copy(bout_hbm, bout, lsem.at[3]),
        pltpu.make_async_copy(query_hbm, query, lsem.at[4]),
    ]
    for copy in local:
        copy.start()

    barrier = pltpu.get_barrier_semaphore()
    for i in range(1, ns):
        pl.semaphore_signal(barrier, inc=1, device_id=(g, lax.rem(s + i, ns)),
                            device_id_type=pl.DeviceIdType.MESH)
    for i in range(1, ng):
        pl.semaphore_signal(barrier, inc=1, device_id=(lax.rem(g + i, ng), s),
                            device_id_type=pl.DeviceIdType.MESH)
    pl.semaphore_wait(barrier, ns - 1 + ng - 1)

    sends = []

    def go(copy):
        copy.start()
        sends.append(copy)

    def gather_start(src, buf, snd, rcv):
        for d in range(1, chips):
            to = lax.rem(chip + d, chips) * 2 + core
            go(remote(src, buf.at[s], snd.at[d], rcv.at[s], (g, to)))
        go(remote(src, buf.at[s], snd.at[0], rcv.at[s], (g, sib)))

    def gather_relay(buf, snd, rcv):
        for d in range(1, chips):
            k = lax.rem(chip + chips - d, chips) * 2 + core
            remote(buf.at[k], buf.at[k], snd.at[0], rcv.at[k], (g, sib)).wait_recv()
            go(remote(buf.at[k], buf.at[k], snd.at[chips + d - 1], rcv.at[k], (g, sib)))

    def gather_end(buf, snd, rcv):
        for d in range(chips):
            k = lax.rem(chip + chips - d, chips) * 2 + 1 - core
            remote(buf.at[k], buf.at[k], snd.at[0], rcv.at[k], (g, sib)).wait_recv()

    for i in range(1, ng):
        go(remote(act, abuf.at[g], a_s.at[i], a_r.at[g], (lax.rem(g + i, ng), s)))
    gather_start(grad, gbuf, g_s, g_r)

    local[0].wait()
    local[1].wait()
    for i in range(1, ng):
        k = lax.rem(g + ng - i, ng)
        remote(act, abuf.at[k], a_s.at[i], a_r.at[k], (k, s)).wait_recv()
    terms = jnp.dot(abuf[...].reshape(tok, -1), bin_v[...], preferred_element_type=F32)
    tsend[...] = terms.reshape(tsend.shape)
    for i in range(1, ns):
        k = lax.rem(s + i, ns)
        go(remote(tsend.at[k], tland.at[s], t_s.at[i], t_r.at[s], (g, k)))
    gather_relay(gbuf, g_s, g_r)
    total = tsend[s]
    for i in range(1, ns):
        k = lax.rem(s + ns - i, ns)
        remote(tsend.at[k], tland.at[k], t_s.at[i], t_r.at[k], (g, k)).wait_recv()
        total = total + tland[k]
    piece[g] = total.astype(BF16)
    for i in range(1, ng):
        go(remote(piece.at[g], piece.at[g], p_s.at[i], p_r.at[g], (lax.rem(g + i, ng), s)))
    gather_end(gbuf, g_s, g_r)
    for copy in local[2:]:
        copy.wait()

    def right(c, where):
        return remote(to_right.at[c], from_left.at[c], zr_s.at[c], zr_r.at[c], (where, s))

    def left(c, where):
        return remote(to_left.at[c], from_right.at[c], zl_s.at[c], zl_r.at[c], (where, s))

    def exchange(k):
        cr = k - SKEW * g

        @pl.when((cr >= 0) & (cr < nch))
        def _():
            @pl.when(g > 0)
            def _():
                right(cr, g).wait_recv()

            @pl.when((g > 0) & (g < ng - 1))
            def _():
                to_right[cr] = (own[cr] + from_left[cr].astype(F32)).astype(BF16)
                right(cr, g + 1).start()

            @pl.when(g == 0)
            def _():
                to_right[cr] = own[cr].astype(BF16)
                right(cr, g + 1).start()

        cl = k - SKEW * (ng - 1 - g)

        @pl.when((cl >= 0) & (cl < nch))
        def _():
            @pl.when(g < ng - 1)
            def _():
                left(cl, g).wait_recv()

            @pl.when((g < ng - 1) & (g > 0))
            def _():
                to_left[cl] = (own[cl] + from_right[cl].astype(F32)).astype(BF16)
                left(cl, g - 1).start()

            @pl.when(g == ng - 1)
            def _():
                to_left[cl] = own[cl].astype(BF16)
                left(cl, g - 1).start()

    def head(k, carry):
        rows = pl.ds(pl.multiple_of(k * ROWS, ROWS), ROWS)
        own[k] = lax.dot_general(
            bout[rows, :], gbuf[...].reshape(tok, -1), NT, preferred_element_type=F32)
        exchange(k)
        return carry

    tail = SKEW * (ng - 1)
    per = -(-nch // tail)

    def rest(k, carry):
        exchange(nch + k)

        def mix(i, carry):
            @pl.when(i < nch)
            def _():
                rows = pl.ds(pl.multiple_of(i * ROWS, ROWS), ROWS)
                mixed[i] = lax.dot_general(
                    query[rows, :], afull[...].reshape(tok, -1), NT,
                    preferred_element_type=F32)

            return carry

        return lax.fori_loop(k * per, k * per + per, mix, carry)

    lax.fori_loop(0, nch // 3, head, 0)
    for i in range(1, ng):
        k = lax.rem(g + ng - i, ng)
        remote(piece.at[k], piece.at[k], p_s.at[i], p_r.at[k], (k, s)).wait_recv()
    for k in range(ng):
        arow[:, k * width:(k + 1) * width] = piece[k]
    afull[s] = arow[...]
    gather_start(arow, afull, f_s, f_r)

    lax.fori_loop(nch // 3, 2 * nch // 3, head, 0)
    gather_relay(afull, f_s, f_r)
    lax.fori_loop(2 * nch // 3, nch, head, 0)
    gather_end(afull, f_s, f_r)
    lax.fori_loop(0, tail, rest, 0)

    def add(k, carry):
        @pl.when(g > 0)
        def _():
            own[k] = own[k] + from_left[k].astype(F32)

        @pl.when(g < ng - 1)
        def _():
            own[k] = own[k] + from_right[k].astype(F32)

        return carry + jnp.sum(mixed[k] * own[k], axis=0, keepdims=True)

    part = lax.fori_loop(0, nch, add, jnp.zeros((1, tok), F32))
    block = tok // ns
    for k in range(ns):
        psend[k] = jnp.broadcast_to(part[:, k * block:(k + 1) * block], (8, block))
    for i in range(1, ns):
        k = lax.rem(s + i, ns)
        go(remote(psend.at[k], pland.at[s], s_s.at[i], s_r.at[s], (g, k)))
    result = psend[s]
    for i in range(1, ns):
        k = lax.rem(s + ns - i, ns)
        remote(psend.at[k], pland.at[k], s_s.at[i], s_r.at[k], (g, k)).wait_recv()
        result = result + pland[k]
    score[...] = result[0:1, :]

    for copy in sends:
        copy.wait_send()

    def drain(k, carry):
        @pl.when(g < ng - 1)
        def _():
            right(k, g + 1).wait_send()

        @pl.when(g > 0)
        def _():
            left(k, g - 1).wait_send()

        return carry

    lax.fori_loop(0, nch, drain, 0)


def local(ng, ns, activations, grad_outputs, basis_in, basis_out, query_grads):
    atok, kin = activations.shape
    gtok, kout = grad_outputs.shape
    width, cols = basis_in.shape[1], basis_out.shape[1]
    eig = query_grads.shape[1]
    tok = atok * ng
    nch = cols // ROWS
    dma = pltpu.SemaphoreType.DMA
    hbm = pl.BlockSpec(memory_space=pl.ANY)
    flops = 2 * tok * (kin * width + kout * cols + eig * cols)
    return pl.pallas_call(
        functools.partial(kernel, ng, ns),
        out_shape=jax.ShapeDtypeStruct((1, gtok), F32),
        in_specs=[hbm] * 5,
        out_specs=pl.BlockSpec(memory_space=pltpu.VMEM),
        scratch_shapes=[
            pltpu.VMEM((kin, width), BF16),
            pltpu.VMEM((cols, kout), BF16),
            pltpu.VMEM((cols, eig), BF16),
            pltpu.VMEM((ng, atok, kin), BF16),
            pltpu.VMEM((ns, gtok, width), F32),
            pltpu.VMEM((ns, gtok, width), F32),
            pltpu.VMEM((ng, gtok, width), BF16),
            pltpu.VMEM((gtok, eig), BF16),
            pltpu.VMEM((ns, gtok, eig), BF16),
            pltpu.VMEM((ns, gtok, kout), BF16),
            pltpu.VMEM((nch, ROWS, tok), F32),
            pltpu.VMEM((nch, ROWS, tok), F32),
        ] + [pltpu.VMEM((nch, ROWS, tok), BF16)] * 4 + [
            pltpu.VMEM((ns, 8, gtok), F32),
            pltpu.VMEM((ns, 8, gtok), F32),
            dma((5,)),
            dma((ng,)), dma((ng,)),
            dma((ns,)), dma((ns,)),
            dma((ng,)), dma((ng,)),
            dma((ns,)), dma((ns,)),
            dma((ns,)), dma((ns,)),
            dma((nch,)), dma((nch,)), dma((nch,)), dma((nch,)),
            dma((ns,)), dma((ns,)),
        ],
        compiler_params=pltpu.CompilerParams(
            collective_id=0, has_side_effects=True, vmem_limit_bytes=60 * 2**20),
        cost_estimate=pl.CostEstimate(
            flops=flops, bytes_accessed=2 * cols * (kout + eig), transcendentals=0),
    )(activations, grad_outputs, basis_in, basis_out.T, query_grads[0].T)


def solution(mesh):
    placed = (
        P("grp", "shard"),
        P("shard", "grp"),
        P("shard", "grp"),
        P("grp", "shard"),
        P("grp", None, "shard"),
    )
    body = functools.partial(local, mesh.shape["grp"], mesh.shape["shard"])
    return jax.shard_map(
        body, mesh=mesh, in_specs=placed, out_specs=P("grp", "shard"), check_vma=False
    )
```

time: 260 us -> 76 us (0.29)
  blocking collectives: 116 us -> 0 us
  waiting for transfers between devices: 106 us -> 0 us
  Pallas kernels: 0 us -> 74.7 us
  matrix products: 21.5 us -> 0 us
  between operations: 13.2 us -> 0.01 us
    psum x2 -> x0, blocking collectives: 116 us -> none  [the longest x1 79.8 us: local(): out_rot = lax.psum(out_terms, 'grp').astype(jnp.bfloat16)]
    pallas_call x0 -> x1, Pallas kernels: none -> 74.7 us  [local(): pl.pallas_call(functools.partial(kernel, ng, ns), out_shape=jax.ShapeDtyp...]
    all_gather x3 -> x0, waiting for transfers between devices: 70.8 us -> none  [the longest x1 69.2 us: local(): full_in = lax.all_gather(basis_in, 'grp', axis=1, tiled=True)]
    unnamed x5 -> x0, waiting for transfers between devices: 35.3 us -> none
    dot_general x3 -> x0, matrix products: 21.5 us -> none  [the longest x1 12.4 us: local(): jnp.dot(lax.all_gather(grad_outputs, 'shard', axis=0, tiled=True), basis_...]
  transfers between devices with their start and end apart: 4 -> 0, of which waited for: 3 -> 0; matrix products, arithmetic and copies ran while one was open for 6% -> 0% of each run, Pallas kernels for 0% -> 0%
where the time goes in v1:
time: 76 us; the launch traced here: 75.9 us
  Pallas kernels  74.7 us (98%)
  local copies, waits for them, and re-layouts  1.19 us (2%)
    pallas_call x1, Pallas kernels, local(): pl.pallas_call(functools.partial(kernel, ng, ns), out_shape=jax.ShapeDtyp...  74.7 us

profile of v1, /device:TPU:0, one launch (start us, length us, event | category | flops | bytes accessed | tf_op | source)
XLA Modules:
  0.0 75.9 jit_solution(6743452936424027242)
XLA Ops:
  0.0 74.7 %shard_map.55 = f32[1,32]{1,0:T(1,128)} custom-call(bf16[64,640]{1,0:T(8,128)(2,1)} %act.1, bf16[32,6912]{1,0:T(8,128)(2,1)} %grad.1, bf16[640,640]{1,0:T(8,128)(2,1)} %bin_hbm.1, bf16[1728,6912]{1,0:T(8,128)(2,1)} %bitcast.4, bf16[1728,2560]{1,0:T(8,128)(2,1)} %bitcast.5), custom_call_target="tpu_custom_call" | custom-call | flops 8589934592 | bytes 32735232 | tf_op jit(solution)/shard_map/pallas_call | solution.py:239
  74.7 1.2 %copy.7 = f32[1,32]{1,0:T(1,128)} copy(f32[1,32]{1,0:T(1,128)} %shard_map.55) | data formatting | bytes 256

commit v2 on v1

--- a/solution.py
+++ b/solution.py
@@ -9,7 +9,7 @@
 
 F32, BF16 = jnp.float32, jnp.bfloat16
 ROWS = 144
-SKEW = 2
+SKEW = 3
 NT = (((1,), (1,)), ((), ()))
 
 

time: 76 us -> 74.8 us (0.984)
  Pallas kernels: 74.7 us -> 73.5 us
    pallas_call x1, Pallas kernels: 74.7 us -> 73.5 us  [local(): pl.pallas_call(functools.partial(kernel, ng, ns), out_shape=jax.ShapeDtyp...]
where the time goes in v2:
time: 74.8 us; the launch traced here: 74.7 us
  Pallas kernels  73.5 us (98%)
  local copies, waits for them, and re-layouts  1.19 us (2%)
    pallas_call x1, Pallas kernels, local(): pl.pallas_call(functools.partial(kernel, ng, ns), out_shape=jax.ShapeDtyp...  73.5 us

profile of v2, /device:TPU:0, one launch (start us, length us, event | category | flops | bytes accessed | tf_op | source)
XLA Modules:
  0.0 74.7 jit_solution(1928097283857369683)
XLA Ops:
  0.0 73.5 %shard_map.55 = f32[1,32]{1,0:T(1,128)} custom-call(bf16[64,640]{1,0:T(8,128)(2,1)} %act.1, bf16[32,6912]{1,0:T(8,128)(2,1)} %grad.1, bf16[640,640]{1,0:T(8,128)(2,1)} %bin_hbm.1, bf16[1728,6912]{1,0:T(8,128)(2,1)} %bitcast.4, bf16[1728,2560]{1,0:T(8,128)(2,1)} %bitcast.5), custom_call_target="tpu_custom_call" | custom-call | flops 8589934592 | bytes 32735232 | tf_op jit(solution)/shard_map/pallas_call | solution.py:239
  73.5 1.2 %copy.7 = f32[1,32]{1,0:T(1,128)} copy(f32[1,32]{1,0:T(1,128)} %shard_map.55) | data formatting | bytes 256
